TPU v7x, 256 devices: a whole 4x4x8 slice. The times are simulated.
256 devices in a mesh: dp: 32 (over z, x), seq: 8 (over y, core).
Axes of the slice: x: 4, y: 4, z: 8, core: 2. Of those that a mesh axis runs over, the one named last changes fastest.
Arguments:
- patches: bfloat16 [32, 98304], P(None, ('dp', 'seq')), may hold values from -12 to 12
- segment_ids: int32 [32, 3072], P('dp'), may hold values from 0 to 15, never falling along the last dimension, each value on 1 to 2304 neighbouring positions
- regroup_plan: int32 [32, 5, 64], P('dp'), may hold values from 0 to 383, as said below
- input_weight: bfloat16 [32, 1280], replicated, may hold values from -1 to 1
- input_bias: float32 [1280], replicated, may hold values from -3 to 3
- skip_weight: bfloat16 [32, 1280], replicated, may hold values from -1 to 1
- hidden_weight: bfloat16 [1280, 1280], replicated, may hold values from -0.15625 to 0.15625
- output_bias: float32 [1280], replicated, may hold values from -3 to 3
- norm_gain: float32 [1280], replicated, may hold values from 0.1 to 1.9
- head_scale: float32 [8], replicated, may hold values from 1 to 4
- qkv_weight: bfloat16 [1280, 3, 640], replicated, may hold values from -0.15625 to 0.15625
- out_weight: bfloat16 [640, 1280], P(None, ('dp', 'seq')), may hold values from -0.25 to 0.25
- cotangent: bfloat16 [98304, 1280], P(('dp', 'seq')), may hold values from -0.3125 to 0.3125
Outputs:
- layer_out: bfloat16 [98304, 1280], P(('dp', 'seq'))
- out_grad: float32 [640, 1280], P(None, ('dp', 'seq'))
Inputs may be any that keep to these rules, and one draw needn't show every extreme that they name: `regroup_plan`: piece s * 8 + d of a window moves rows of source shard s to destination shard d: one piece for each pair, each moving one row or more. The pieces of a window cover each of the 384 rows of every source shard once and each of the 384 rows of every destination shard once. A piece moves at most 96 rows, and in every window some piece moves exactly 96. `segment_ids`: series ids never fall along a window's positions; one series of each window has exactly 2304 positions.
All inputs are finite; a program needn't handle non-finite values.
Results may differ from a plain program's by a relative error of at most 0.015.
Values may be sent and summed in bfloat16 or wider, within the bound.
A program may use at most 64 MiB of HBM per device.

v0:
```python
import math
import jax
import jax.numpy as jnp
from jax import lax
from jax.sharding import PartitionSpec as P

HD = 80
EPSILON = 1e-06
CONTRACT_FIRST = (((0,), (0,)), ((), ()))


def row_norm(values):
    return values * lax.rsqrt(jnp.mean(values * values, axis=-1, keepdims=True) + EPSILON)


def place_table(plan_rows, shard_rows, shard_count):
    source = plan_rows[0]
    first_row = plan_rows[1]
    row_count = plan_rows[2]
    target = plan_rows[3]
    offset_row = plan_rows[4]
    window_len = shard_rows * shard_count
    loader_row = jnp.arange(window_len, dtype=jnp.int32)
    begin_row = source * shard_rows + first_row
    inside = (loader_row[None, :] >= begin_row[:, None]) & (
        loader_row[None, :] < (begin_row + row_count)[:, None]
    )
    earlier = (
        (source[:, None] == source[None, :])
        & (target[:, None] == target[None, :])
        & (first_row[None, :] < first_row[:, None])
    )
    base_rank = jnp.sum(jnp.where(earlier, row_count[None, :], 0), axis=1)
    position = jnp.sum(
        jnp.where(
            inside, (target * shard_rows + offset_row - begin_row)[:, None] + loader_row[None, :], 0
        ),
        axis=0,
    )
    slot_rank = jnp.sum(
        jnp.where(inside, (base_rank - begin_row)[:, None] + loader_row[None, :], 0), axis=0
    )
    return (position, slot_rank)


def patch_block(columns, input_weight, input_bias, skip_weight, hidden_weight, output_bias):
    pre_act = (
        lax.dot_general(columns, input_weight, CONTRACT_FIRST, preferred_element_type=jnp.float32)
        + input_bias
    )
    hidden = jax.nn.silu(pre_act).astype(jnp.bfloat16)
    skipped = lax.dot_general(
        columns, skip_weight, CONTRACT_FIRST, preferred_element_type=jnp.float32
    )
    embedded = (
        jnp.dot(hidden, hidden_weight, preferred_element_type=jnp.float32) + skipped + output_bias
    )
    return embedded.astype(jnp.bfloat16)


def per_device(
    patches,
    segment_ids,
    regroup_plan,
    input_weight,
    input_bias,
    skip_weight,
    hidden_weight,
    output_bias,
    norm_gain,
    head_scale,
    qkv_weight,
    out_weight,
    cotangent,
):
    shard_count = lax.axis_size("seq")
    shard_index = lax.axis_index("seq")
    shard_rows = cotangent.shape[0]
    model_width = cotangent.shape[1]
    window_len = shard_rows * shard_count
    capacity = 2 * shard_rows // shard_count
    position, slot_rank = place_table(regroup_plan[0], shard_rows, shard_count)
    loader_row = jnp.arange(window_len, dtype=jnp.int32)
    own_rows = lax.dynamic_slice_in_dim(position, shard_index * shard_rows, shard_rows, 0)
    own_ranks = lax.dynamic_slice_in_dim(slot_rank, shard_index * shard_rows, shard_rows, 0)
    send_slot = own_rows // shard_rows * capacity + own_ranks
    send_table = (
        jnp.full((shard_count * capacity,), shard_rows, jnp.int32)
        .at[send_slot]
        .set(jnp.arange(shard_rows, dtype=jnp.int32))
    )
    landing = jnp.where(position // shard_rows == shard_index, position % shard_rows, shard_rows)
    receive_table = (
        jnp.zeros((shard_rows,), jnp.int32)
        .at[landing]
        .set(loader_row // shard_rows * capacity + slot_rank, mode="drop")
    )
    local_embed = patch_block(
        patches, input_weight, input_bias, skip_weight, hidden_weight, output_bias
    )
    padded = jnp.concatenate([local_embed, jnp.zeros((1, model_width), jnp.bfloat16)], axis=0)
    arrived = lax.all_to_all(padded[send_table], "seq", split_axis=0, concat_axis=0, tiled=True)
    embedded = arrived[receive_table]
    normed = (row_norm(embedded.astype(jnp.float32)) * norm_gain).astype(jnp.bfloat16)
    projected = jnp.dot(
        normed, qkv_weight.reshape(model_width, -1), preferred_element_type=jnp.float32
    )
    projected = projected.astype(jnp.bfloat16).reshape(shard_rows, 3, -1)
    head_rows = lax.all_to_all(projected, "seq", split_axis=2, concat_axis=0, tiled=True)
    local_width = head_rows.shape[2]
    local_heads = local_width // HD
    queries = row_norm(
        head_rows[:, 0].reshape(window_len, local_heads, HD).astype(jnp.float32)
    ).astype(jnp.bfloat16)
    key_rows = row_norm(
        head_rows[:, 1].reshape(window_len, local_heads, HD).astype(jnp.float32)
    ).astype(jnp.bfloat16)
    value_rows = head_rows[:, 2].reshape(window_len, local_heads, HD)
    factor = lax.dynamic_slice_in_dim(head_scale, shard_index * local_heads, local_heads, 0) * (
        1.0 / math.sqrt(HD)
    )
    segment_row = segment_ids[0]
    block_len = min(512, window_len)
    block_count = window_len // block_len
    pieces = []
    for block_index in range(block_count):
        query_first = block_index * block_len
        query_part = queries[query_first : query_first + block_len]
        query_pos = query_first + jnp.arange(block_len, dtype=jnp.int32)
        query_seg = segment_row[query_first : query_first + block_len]
        key_len = query_first + block_len
        key_part = lax.slice_in_dim(key_rows, 0, key_len, axis=0)
        value_part = lax.slice_in_dim(value_rows, 0, key_len, axis=0)
        key_seg = lax.slice_in_dim(segment_row, 0, key_len, axis=0)
        key_pos = jnp.arange(key_len, dtype=jnp.int32)
        scores = (
            jnp.einsum("qhd,khd->hqk", query_part, key_part, preferred_element_type=jnp.float32)
            * factor[:, None, None]
        )
        allowed = (query_seg[:, None] == key_seg[None, :]) & (
            key_pos[None, :] <= query_pos[:, None]
        )
        weights = jnp.where(allowed[None], jnp.exp(scores), 0.0)
        summed = jnp.einsum(
            "hqk,khd->qhd",
            weights.astype(jnp.bfloat16),
            value_part,
            preferred_element_type=jnp.float32,
        )
        summed, denominator = (summed, jnp.sum(weights, axis=-1))
        pieces.append(
            (summed / jnp.transpose(denominator)[:, :, None]).reshape(block_len, local_width)
        )
    attended = jnp.concatenate(pieces, axis=0).astype(jnp.bfloat16)
    returned = lax.all_to_all(attended, "seq", split_axis=0, concat_axis=1, tiled=True)
    branch = jnp.dot(
        returned,
        lax.all_gather(out_weight, ("dp", "seq"), axis=1, tiled=True),
        preferred_element_type=jnp.float32,
    )
    layer_out = (embedded.astype(jnp.float32) + branch).astype(jnp.bfloat16)
    grad_term = lax.dot_general(
        returned, cotangent, CONTRACT_FIRST, preferred_element_type=jnp.float32
    )
    out_grad = lax.psum_scatter(grad_term, ("dp", "seq"), scatter_dimension=1, tiled=True)
    return (layer_out, out_grad)


def solution(mesh):
    placed = (
        P(None, ("dp", "seq")),
        P("dp", None),
        P("dp", None, None),
        P(),
        P(),
        P(),
        P(),
        P(),
        P(),
        P(),
        P(),
        P(None, ("dp", "seq")),
        P(("dp", "seq"), None),
    )
    return jax.shard_map(
        per_device,
        mesh=mesh,
        in_specs=placed,
        out_specs=(P(("dp", "seq"), None), P(None, ("dp", "seq"))),
        check_vma=False,
    )
```

profile of v0, /device:TPU:2, one launch (start us, length us, event | category | flops | bytes accessed | tf_op | source)
XLA Modules:
  0.0 472.5 jit_solution(12129723158445891963)
XLA Ops:
  7.2 0.9 slice_bitcast_fusion.37
  8.0 0.2 select_reduce_fusion.2
  8.2 0.7 fusion.119
  8.9 0.7 fusion.118
  9.6 0.4 select_reduce_fusion.1
  10.1 2.9 scatter_custom_fusion
  13.1 4.2 fusion.23
  17.3 2.0 fusion.9
  19.3 1.0 concatenate.7
  20.3 6.5 %gather_fusion = bf16[768,1280]{1,0:T(8,128)(2,1)} fusion(bf16[385,1280]{1,0:T(8,128)(2,1)} %concatenate.7, s32[1024]{0:T(1024)S(1)} %pad_clamp_fusion.1), kind=kCustom, calls=%fused_computation | custom fusion | bytes 3935232 | tf_op jit(solution)/shard_map/gather | solution.py:102
  26.8 4.5 all-to-all-start
  31.3 8.2 %copy.25 = bf16[1280,3,640]{0,2,1:T(8,128)(2,1)} copy(bf16[1280,3,640]{2,0,1:T(8,128)(2,1)} %param.23) | data formatting | bytes 9830400 | tf_op args[10]
  39.6 11.9 %scatter_custom_fusion.1 = s32[384]{0:T(512)S(1)} fusion(s32[3072]{0:T(1024)S(1)} %bitcast.265, s32[3072]{0:T(1024)S(1)} %get-tuple-element.36, s32[]{:T(128)} %constant.25.clone.1), kind=kCustom, calls=%fused_computation.154 | custom fusion | bytes 1540 | tf_op jit(solution)/shard_map/scatter | solution.py:96
  51.6 5.6 %all-to-all-done = bf16[8,96,1280]{2,1,0:T(8,128)(2,1)} async-done(((bf16[8,96,1280]{2,1,0:T(8,128)(2,1)}), bf16[8,96,1280]{2,1,0:T(8,128)(2,1)}, u32[]{:S(2)}, u32[]{:S(2)}) %all-to-all-start) | async-done | bytes 1966112 | tf_op jit(solution)/shard_map/all_to_all | solution.py:102
  57.2 5.6 %gather_fusion.1 = bf16[384,1280]{1,0:T(8,128)(2,1)} fusion(bf16[768,1280]{1,0:T(8,128)(2,1)} %bitcast.6, s32[1024]{0:T(1024)S(1)} %pad_clamp_fusion), kind=kCustom, calls=%fused_computation.1 | custom fusion | bytes 1967616 | tf_op jit(solution)/shard_map/gather | solution.py:103
  62.8 1.5 fusion.16
  64.3 6.2 %convolution_convert_fusion = bf16[384,1920]{1,0:T(8,128)(2,1)} fusion(bf16[1280,1920]{0,1:T(8,128)(2,1)} %bitcast.255, bf16[384,1280]{1,0:T(8,128)(2,1)} %gather_fusion.1, f32[1280]{0:T(1024)S(1)} %copy-done.7, f32[384]{0:T(512)S(1)} %add_rsqrt_fusion.2), kind=kOutput, calls=%fused_computation.27 | convolution fusion | flops 1890140160 | bytes 7379456 | tf_op jit(solution)/shard_map/dot_general | solution.py:105
  70.5 2.6 copy.26
  73.0 3.9 copy.27
  77.0 4.5 all-to-all-start.1
  81.5 0.7 all-gather.3.cloned.1.call-update
  82.2 0.3 all-reduce.4.cloned.1.call-start
  82.4 0.6 dynamic_slice.11
  83.8 23.4 %all-to-all-done.1 = bf16[384,3,640]{0,1,2:T(4,128)(2,1)} async-done(((bf16[384,3,640]{0,1,2:T(4,128)(2,1)}), bf16[384,3,640]{0,1,2:T(4,128)(2,1)}, u32[]{:S(2)}, u32[]{:S(2)}) %all-to-all-start.1) | async-done | bytes 1474592 | tf_op jit(solution)/shard_map/all_to_all | solution.py:109
  107.3 1.7 copy.28
  109.0 0.3 copy.32
  109.3 0.2 fusion.94
  109.5 0.2 fusion.95
  109.7 0.4 fusion.121
  110.2 0.2 fusion.91
  110.4 0.9 fusion.122
  111.4 1.4 fusion.123
  112.7 0.5 fusion.87
  113.2 0.6 fusion.63
  113.8 1.9 fusion.124
  115.7 0.8 fusion.81
  116.5 2.3 fusion.125
  118.8 0.9 fusion.75
  119.8 2.7 fusion.126
  122.5 1.1 fusion.69
  123.6 12.4 %all_to_all.46 = bf16[8,384,80]{1,2,0:T(8,128)(2,1)S(1)} all-to-all(bf16[8,384,80]{1,2,0:T(8,128)(2,1)S(1)} %bitcast.258), channel_id=1, replica_groups=mesh['dp'=32,'seq'=8] {'seq'}, dimensions={0} | all-to-all | bytes 983040 | tf_op jit(solution)/shard_map/all_to_all | solution.py:155
  136.1 0.8 copy-done.1
  136.9 2.9 fusion.127
  139.7 54.4 %all-gather.3.cloned.1.call-done = bf16[256,5,640]{2,1,0:T(8,128)(2,1)} async-done(((bf16[1,5,640]{2,1,0:T(8,128)(2,1)}), bf16[256,5,640]{2,1,0:T(8,128)(2,1)}) %all-gather.3.cloned.1.call-update) | async-done | bytes 1638416 | tf_op jit(solution)/shard_map/all_gather | solution.py:158
  194.1 4.1 reshape.456
  198.2 3.8 fusion.10
  202.0 262.3 %all-reduce.4.cloned.1.call-done = f32[640,1280]{0,1:T(8,128)} async-done(((f32[640,1280]{0,1:T(8,128)}), f32[640,1280]{0,1:T(8,128)}) %all-reduce.4.cloned.1.call-update) | async-done | bytes 3276816
  464.3 1.4 constant_dynamic-slice_fusion
  (44 shorter events, 0.5 us)
Async XLA Ops:
  7.2 5.9 %copy-start = (bf16[1280,1280]{1,0:T(8,128)(2,1)S(1)}, bf16[1280,1280]{1,0:T(8,128)(2,1)}, u32[]{:S(2)}) copy-start(bf16[1280,1280]{1,0:T(8,128)(2,1)} %param.19) | copy-start | bytes 9830404
  13.1 4.2 copy-start.4
  13.1 4.2 copy-start.5
  13.1 4.2 copy-start.6
  26.8 30.4 %all-to-all-start = ((bf16[8,96,1280]{2,1,0:T(8,128)(2,1)}), bf16[8,96,1280]{2,1,0:T(8,128)(2,1)}, u32[]{:S(2)}, u32[]{:S(2)}) async-start(bf16[8,96,1280]{2,1,0:T(8,128)(2,1)} %bitcast.252), calls=%async_computation | async-start | bytes 3932160 | tf_op jit(solution)/shard_map/all_to_all | solution.py:102
  57.2 7.1 %copy-start.7 = (f32[1280]{0:T(1024)S(1)}, f32[1280]{0:T(1024)}, u32[]{:S(2)}) copy-start(f32[1280]{0:T(1024)} %param.21) | copy-start | bytes 15364
  76.9 5.5 %copy-start.8 = (f32[8]{0:T(128)S(1)}, f32[8]{0:T(128)}, u32[]{:S(2)}) copy-start(f32[8]{0:T(128)} %param.22) | copy-start | bytes 100
  76.9 6.8 %copy-start.3 = (s32[1,3072]{1,0:T(1,128)S(1)}, s32[1,3072]{1,0:T(1,128)}, u32[]{:S(2)}) copy-start(s32[1,3072]{1,0:T(1,128)} %param.14) | copy-start | bytes 36868
  77.0 30.3 %all-to-all-start.1 = ((bf16[384,3,640]{0,1,2:T(4,128)(2,1)}), bf16[384,3,640]{0,1,2:T(4,128)(2,1)}, u32[]{:S(2)}, u32[]{:S(2)}) async-start(bf16[384,3,640]{0,1,2:T(4,128)(2,1)} %copy.27), calls=%async_computation.1 | async-start | bytes 3932160 | tf_op jit(solution)/shard_map/all_to_all | solution.py:109
  81.4 112.7 %all-gather.3.cloned.1.call-start = ((), (), s32[]{:S(2)}) async-start(), calls=%async_computation.3 | async-start | bytes 2631680 | tf_op jit(solution)/shard_map/all_gather | solution.py:158
  82.2 382.1 %all-reduce.4.cloned.1.call-start = ((), (), s32[]{:S(2)}) async-start(), calls=%async_computation.4 | async-start | bytes 6553600
  109.7 0.7 slice-start
  112.7 1.1 slice-start.1
  122.5 14.4 %copy-start.2 = (bf16[384,1280]{1,0:T(8,128)(2,1)S(1)}, bf16[384,1280]{1,0:T(8,128)(2,1)}, u32[]{:S(2)}) copy-start(bf16[384,1280]{1,0:T(8,128)(2,1)} %param.25) | copy-start | bytes 2949124
  136.1 0.8 copy-start.1
Sparse Core Ops, SparseCore 0:
  86.0 108.0 all-gather.2
  199.6 264.6 all-reduce.3
where the time goes:
time: 474 us; the launch traced here: 473 us
  waiting for transfers between devices  346 us (73%)
  local copies, waits for them, and re-layouts  52.6 us (11%)
  matrix products  32.7 us (7%)
  between operations  15 us (3%)
  blocking collectives  12.4 us (3%)
  starting transfers between devices  9.23 us (2%)
    unnamed x3, waiting for transfers between devices  263 us
    all_gather x1, waiting for transfers between devices, per_device(): lax.all_gather(out_weight, ('dp', 'seq'), axis=1, tiled=True)  54.4 us
    all_to_all x1, waiting for transfers between devices, per_device(): lax.all_to_all(projected, 'seq', split_axis=2, concat_axis=0, tiled=True)  23.4 us
    unnamed x21, local copies, waits for them, and re-layouts  14.5 us
    all_to_all x1, blocking collectives, per_device(): lax.all_to_all(attended, 'seq', split_axis=0, concat_axis=1, tiled=True)  12.4 us
    scatter x1, local copies, waits for them, and re-layouts, per_device(): receive_table = jnp.zeros((shard_rows,), jnp.int32).at[landing].set(loade...  11.9 us
    dot_general x6, matrix products, per_device(): jnp.einsum('qhd,khd->hqk', query_part, key_part, preferred_element_type=j...  9.69 us
  transfers between devices with their start and end apart: 4, of which 4 were waited for; matrix products, arithmetic and copies ran while one was open for 10% of the time, Pallas kernels for 0%

commit v1 on v0

--- a/solution.py
+++ b/solution.py
@@ -3,10 +3,23 @@
 import jax.numpy as jnp
 from jax import lax
 from jax.sharding import PartitionSpec as P
+from jax.lax import axis_index, axis_size, ppermute
 
 HD = 80
 EPSILON = 1e-06
 CONTRACT_FIRST = (((0,), (0,)), ((), ()))
+
+
+def update_digits(matrix, dim_k, arr):
+    y_new, finding = (matrix.shape[:dim_k], matrix.shape[dim_k + 1 :])
+    w_next = matrix.reshape(*y_new, arr, -1, *finding)
+    return jnp.moveaxis(w_next, dim_k, 0)
+
+
+def deliver_leaf(frame_in, k_dim):
+    carry_in = list(frame_in.shape[1:])
+    carry_in[k_dim] *= frame_in.shape[0]
+    return jnp.moveaxis(frame_in, 0, k_dim).reshape(carry_in)
 
 
 def row_norm(values):
@@ -106,7 +119,18 @@
         normed, qkv_weight.reshape(model_width, -1), preferred_element_type=jnp.float32
     )
     projected = projected.astype(jnp.bfloat16).reshape(shard_rows, 3, -1)
-    head_rows = lax.all_to_all(projected, "seq", split_axis=2, concat_axis=0, tiled=True)
+    e_next = axis_size("seq")
+    moved, mat_out = (e_next, axis_index("seq"))
+    spare = update_digits(projected, 2, moved)
+    ledger = [spare[mat_out]]
+    ii = 1
+    while ii < moved:
+        y1 = spare[mat_out ^ ii]
+        u1 = ppermute(y1, "seq", [(kk, kk ^ ii) for kk in range(moved)])
+        ledger.append(u1)
+        ii = ii + 1
+    spare = jnp.stack(ledger)[mat_out ^ jnp.arange(moved)]
+    head_rows = deliver_leaf(spare, 0)
     local_width = head_rows.shape[2]
     local_heads = local_width // HD
     queries = row_norm(

time: 474 us -> 428 us (0.903)
  waiting for transfers between devices: 346 us -> 290 us
  local copies, waits for them, and re-layouts: 52.6 us -> 59.3 us
    all_gather x1, waiting for transfers between devices: 54.4 us -> 9.75 us  [per_device(): lax.all_gather(out_weight, ('dp', 'seq'), axis=1, tiled=True)]
    all_to_all x1 -> x0, waiting for transfers between devices: 23.4 us -> none  [per_device(): lax.all_to_all(projected, 'seq', split_axis=2, concat_axis=0, tiled=True)]
    ppermute x0 -> x7, waiting for transfers between devices: none -> 13 us  [per_device(): u1 = ppermute(y1, 'seq', [(kk, kk ^ ii) for kk in range(moved)])]
    ppermute x0 -> x7, starting transfers between devices: none -> 8.14 us  [per_device(): u1 = ppermute(y1, 'seq', [(kk, kk ^ ii) for kk in range(moved)])]
    unnamed x21 -> x28, local copies, waits for them, and re-layouts: 14.5 us -> 20.3 us
  transfers between devices with their start and end apart: 4 -> 10, of which waited for: 4 -> 7; matrix products, arithmetic and copies ran while one was open for 10% -> 17% of each run, Pallas kernels for 0% -> 0%
where the time goes in v1:
time: 428 us; the launch traced here: 427 us
  waiting for transfers between devices  290 us (68%)
  local copies, waits for them, and re-layouts  59.3 us (14%)
  matrix products  32.7 us (8%)
  between operations  15.1 us (4%)
  blocking collectives  13.5 us (3%)
  starting transfers between devices  12.7 us (3%)
    unnamed x3, waiting for transfers between devices  263 us
    unnamed x28, local copies, waits for them, and re-layouts  20.3 us
    all_to_all x1, blocking collectives, per_device(): lax.all_to_all(attended, 'seq', split_axis=0, concat_axis=1, tiled=True)  13.5 us
    ppermute x7, waiting for transfers between devices, per_device(): u1 = ppermute(y1, 'seq', [(kk, kk ^ ii) for kk in range(moved)])  13 us
    scatter x1, local copies, waits for them, and re-layouts, per_device(): receive_table = jnp.zeros((shard_rows,), jnp.int32).at[landing].set(loade...  11.8 us
    all_gather x1, waiting for transfers between devices, per_device(): lax.all_gather(out_weight, ('dp', 'seq'), axis=1, tiled=True)  9.75 us
    dot_general x6, matrix products, per_device(): jnp.einsum('qhd,khd->hqk', query_part, key_part, preferred_element_type=j...  9.69 us
  transfers between devices with their start and end apart: 10, of which 7 were waited for; matrix products, arithmetic and copies ran while one was open for 17% of the time, Pallas kernels for 0%

profile of v1, /device:TPU:2, one launch (start us, length us, event | category | flops | bytes accessed | tf_op | source)
XLA Modules:
  0.0 427.0 jit_solution(4654660891417229234)
XLA Ops:
  7.2 0.9 slice_bitcast_fusion.37
  8.9 0.7 fusion.119
  10.1 2.9 scatter_custom_fusion
  13.1 4.2 fusion.23
  17.3 2.0 fusion.9
  19.3 1.0 concatenate.7
  20.3 6.5 %gather_fusion = bf16[768,1280]{1,0:T(8,128)(2,1)} fusion(bf16[385,1280]{1,0:T(8,128)(2,1)} %concatenate.7, s32[1024]{0:T(1024)S(1)} %pad_clamp_fusion.2), kind=kCustom, calls=%fused_computation | custom fusion | bytes 3935232 | tf_op jit(solution)/shard_map/gather | solution.py:115
  26.8 4.5 %all-to-all-start = ((bf16[8,96,1280]{2,1,0:T(8,128)(2,1)}), bf16[8,96,1280]{2,1,0:T(8,128)(2,1)}, u32[]{:S(2)}, u32[]{:S(2)}) async-start(bf16[8,96,1280]{2,1,0:T(8,128)(2,1)} %bitcast.282), calls=%async_computation | async-start | bytes 3932160 | tf_op jit(solution)/shard_map/all_to_all | solution.py:115
  32.3 8.2 %copy.26 = bf16[1280,3,640]{0,2,1:T(8,128)(2,1)} copy(bf16[1280,3,640]{2,0,1:T(8,128)(2,1)} %param.23) | data formatting | bytes 9830400 | tf_op args[10]
  41.7 11.8 %scatter_custom_fusion.1 = s32[384]{0:T(512)S(1)} fusion(s32[3072]{0:T(1024)S(1)} %bitcast.295, s32[3072]{0:T(1024)S(1)} %get-tuple-element.43, s32[]{:T(128)} %constant.31.clone.1), kind=kCustom, calls=%fused_computation.172 | custom fusion | bytes 1540 | tf_op jit(solution)/shard_map/scatter | solution.py:109
  53.7 3.6 all-to-all-done
  57.3 5.6 %gather_fusion.1 = bf16[384,1280]{1,0:T(8,128)(2,1)} fusion(bf16[768,1280]{1,0:T(8,128)(2,1)} %bitcast.6, s32[1024]{0:T(1024)S(1)} %pad_clamp_fusion.1), kind=kCustom, calls=%fused_computation.1 | custom fusion | bytes 1967616 | tf_op jit(solution)/shard_map/gather | solution.py:116
  62.9 1.5 fusion.16
  64.3 6.1 %convolution_convert_fusion = bf16[384,1920]{1,0:T(8,128)(2,1)} fusion(bf16[1280,1920]{0,1:T(8,128)(2,1)} %bitcast.285, bf16[384,1280]{1,0:T(8,128)(2,1)} %gather_fusion.1, f32[1280]{0:T(1024)S(1)} %copy-done.7, f32[384]{0:T(512)S(1)} %add_rsqrt_fusion.2), kind=kOutput, calls=%fused_computation.28 | convolution fusion | flops 1890140160 | bytes 7379456 | tf_op jit(solution)/shard_map/dot_general | solution.py:118
  70.5 2.6 copy.27
  73.0 1.5 dynamic-slice_bitcast_fusion
  74.6 0.8 collective-permute-start.1
  75.5 1.0 collective-permute-start.2
  76.5 1.1 collective-permute-start.3
  77.5 2.4 collective-permute-start.4
  79.9 1.6 bitcast_dynamic-update-slice_fusion.7
  81.5 1.2 collective-permute-start.5
  83.4 1.6 collective-permute-start.6
  85.0 0.7 bitcast_dynamic-update-slice_fusion.5
  85.7 0.7 bitcast_dynamic-update-slice_fusion.4
  86.4 4.7 %collective-permute-done.3 = bf16[384,3,80]{0,2,1:T(8,128)(2,1)S(1)} collective-permute-done((bf16[384,3,80]{0,2,1:T(8,128)(2,1)S(1)}, bf16[384,3,80]{0,2,1:T(8,128)(2,1)S(1)}, u32[]{:S(2)}, u32[]{:S(2)}) %collective-permute-start.3) | collective-permute-done | bytes 184352 | tf_op jit(solution)/shard_map/ppermute | solution.py:129
  91.2 0.7 bitcast_dynamic-update-slice_fusion.3
  91.9 1.8 collective-permute-done.4
  94.4 3.7 collective-permute-done.5
  98.8 2.8 collective-permute-done.6
  102.2 3.2 gather_fusion.2
  105.5 1.6 copy.31
  108.2 0.9 fusion.123
  109.2 1.4 fusion.124
  111.6 1.9 fusion.125
  113.6 0.8 fusion.81
  114.3 2.3 fusion.126
  116.7 0.9 fusion.75
  117.6 2.7 fusion.127
  120.3 1.1 fusion.69
  121.4 13.5 %all_to_all.28 = bf16[8,384,80]{1,2,0:T(8,128)(2,1)S(1)} all-to-all(bf16[8,384,80]{1,2,0:T(8,128)(2,1)S(1)} %bitcast.288), channel_id=1, replica_groups=mesh['dp'=32,'seq'=8] {'seq'}, dimensions={0} | all-to-all | bytes 983040 | tf_op jit(solution)/shard_map/all_to_all | solution.py:179
  134.9 0.8 copy-done.1
  135.7 2.9 fusion.128
  138.6 9.7 %all-gather.3.cloned.1.call-done = bf16[256,5,640]{2,1,0:T(8,128)(2,1)} async-done(((bf16[1,5,640]{2,1,0:T(8,128)(2,1)}), bf16[256,5,640]{2,1,0:T(8,128)(2,1)}) %all-gather.3.cloned.1.call-update) | async-done | bytes 1638416 | tf_op jit(solution)/shard_map/all_gather | solution.py:182
  148.4 4.1 reshape.495
  152.5 3.8 fusion.10
  156.2 262.6 %all-reduce.4.cloned.1.call-done = f32[640,1280]{0,1:T(8,128)} async-done(((f32[640,1280]{0,1:T(8,128)}), f32[640,1280]{0,1:T(8,128)}) %all-reduce.4.cloned.1.call-update) | async-done | bytes 3276816
  418.8 1.4 constant_dynamic-slice_fusion
  (66 shorter events, 8.1 us)
Async XLA Ops:
  7.2 5.9 %copy-start = (bf16[1280,1280]{1,0:T(8,128)(2,1)S(1)}, bf16[1280,1280]{1,0:T(8,128)(2,1)}, u32[]{:S(2)}) copy-start(bf16[1280,1280]{1,0:T(8,128)(2,1)} %param.19) | copy-start | bytes 9830404
  13.1 4.2 copy-start.4
  13.1 4.2 copy-start.5
  13.1 4.2 copy-start.6
  26.8 30.4 %all-to-all-start = ((bf16[8,96,1280]{2,1,0:T(8,128)(2,1)}), bf16[8,96,1280]{2,1,0:T(8,128)(2,1)}, u32[]{:S(2)}, u32[]{:S(2)}) async-start(bf16[8,96,1280]{2,1,0:T(8,128)(2,1)} %bitcast.282), calls=%async_computation | async-start | bytes 3932160 | tf_op jit(solution)/shard_map/all_to_all | solution.py:115
  31.3 117.1 %all-gather.3.cloned.1.call-start = ((), (), s32[]{:S(2)}) async-start(), calls=%async_computation.2 | async-start | bytes 2631680 | tf_op jit(solution)/shard_map/all_gather | solution.py:182
  32.0 386.8 %all-reduce.4.cloned.1.call-start = ((), (), s32[]{:S(2)}) async-start(), calls=%async_computation.3 | async-start | bytes 6553600
  32.2 8.2 %copy-start.8 = (f32[8]{0:T(128)S(1)}, f32[8]{0:T(128)}, u32[]{:S(2)}) copy-start(f32[8]{0:T(128)} %param.22) | copy-start | bytes 100
  32.2 21.4 %copy-start.3 = (s32[1,3072]{1,0:T(1,128)S(1)}, s32[1,3072]{1,0:T(1,128)}, u32[]{:S(2)}) copy-start(s32[1,3072]{1,0:T(1,128)} %param.14) | copy-start | bytes 36868
  57.2 7.1 %copy-start.7 = (f32[1280]{0:T(1024)S(1)}, f32[1280]{0:T(1024)}, u32[]{:S(2)}) copy-start(f32[1280]{0:T(1024)} %param.21) | copy-start | bytes 15364
  74.5 7.0 %collective-permute-start = (bf16[384,3,80]{0,2,1:T(8,128)(2,1)S(1)}, bf16[384,3,80]{0,2,1:T(8,128)(2,1)S(1)}, u32[]{:S(2)}, u32[]{:S(2)}) collective-permute-start(bf16[384,3,80]{0,2,1:T(8,128)(2,1)S(1)} %get-tuple-element.16), channel_id=1, source_target_pairs={{0,1},{1,0},{2,3},{3,2},{4,5},{5,4},{6,7},{7,6},{8,9},{9,8},{10,11... | collective-permute-start | bytes 552968 | tf_op jit(solution)/shard_map/ppermute | solution.py:129
  74.6 8.7 %collective-permute-start.1 = (bf16[384,3,80]{0,2,1:T(8,128)(2,1)S(1)}, bf16[384,3,80]{0,2,1:T(8,128)(2,1)S(1)}, u32[]{:S(2)}, u32[]{:S(2)}) collective-permute-start(bf16[384,3,80]{0,2,1:T(8,128)(2,1)S(1)} %get-tuple-element.15), channel_id=1, source_target_pairs={{0,2},{1,3},{2,0},{3,1},{4,6},{5,7},{6,4},{7,5},{8,10},{9,11},{10,... | collective-permute-start | bytes 552968 | tf_op jit(solution)/shard_map/ppermute | solution.py:129
  75.5 10.2 %collective-permute-start.2 = (bf16[384,3,80]{0,2,1:T(8,128)(2,1)S(1)}, bf16[384,3,80]{0,2,1:T(8,128)(2,1)S(1)}, u32[]{:S(2)}, u32[]{:S(2)}) collective-permute-start(bf16[384,3,80]{0,2,1:T(8,128)(2,1)S(1)} %get-tuple-element.14), channel_id=1, source_target_pairs={{0,3},{1,2},{2,1},{3,0},{4,7},{5,6},{6,5},{7,4},{8,11},{9,10},{10,... | collective-permute-start | bytes 552968 | tf_op jit(solution)/shard_map/ppermute | solution.py:129
  76.5 14.7 %collective-permute-start.3 = (bf16[384,3,80]{0,2,1:T(8,128)(2,1)S(1)}, bf16[384,3,80]{0,2,1:T(8,128)(2,1)S(1)}, u32[]{:S(2)}, u32[]{:S(2)}) collective-permute-start(bf16[384,3,80]{0,2,1:T(8,128)(2,1)S(1)} %get-tuple-element.13), channel_id=1, source_target_pairs={{0,4},{1,5},{2,6},{3,7},{4,0},{5,1},{6,2},{7,3},{8,12},{9,13},{10,... | collective-permute-start | bytes 552968 | tf_op jit(solution)/shard_map/ppermute | solution.py:129
  77.5 16.1 %collective-permute-start.4 = (bf16[384,3,80]{0,2,1:T(8,128)(2,1)S(1)}, bf16[384,3,80]{0,2,1:T(8,128)(2,1)S(1)}, u32[]{:S(2)}, u32[]{:S(2)}) collective-permute-start(bf16[384,3,80]{0,2,1:T(8,128)(2,1)S(1)} %get-tuple-element.12), channel_id=1, source_target_pairs={{0,5},{1,4},{2,7},{3,6},{4,1},{5,0},{6,3},{7,2},{8,13},{9,12},{10,... | collective-permute-start | bytes 552968 | tf_op jit(solution)/shard_map/ppermute | solution.py:129
  81.5 16.5 %collective-permute-start.5 = (bf16[384,3,80]{0,2,1:T(8,128)(2,1)S(1)}, bf16[384,3,80]{0,2,1:T(8,128)(2,1)S(1)}, u32[]{:S(2)}, u32[]{:S(2)}) collective-permute-start(bf16[384,3,80]{0,2,1:T(8,128)(2,1)S(1)} %get-tuple-element.11), channel_id=1, source_target_pairs={{0,6},{1,7},{2,4},{3,5},{4,2},{5,3},{6,0},{7,1},{8,14},{9,15},{10,... | collective-permute-start | bytes 552968 | tf_op jit(solution)/shard_map/ppermute | solution.py:129
  83.4 18.1 %collective-permute-start.6 = (bf16[384,3,80]{0,2,1:T(8,128)(2,1)S(1)}, bf16[384,3,80]{0,2,1:T(8,128)(2,1)S(1)}, u32[]{:S(2)}, u32[]{:S(2)}) collective-permute-start(bf16[384,3,80]{0,2,1:T(8,128)(2,1)S(1)} %get-tuple-element.10), channel_id=1, source_target_pairs={{0,7},{1,6},{2,5},{3,4},{4,3},{5,2},{6,1},{7,0},{8,15},{9,14},{10,... | collective-permute-start | bytes 552968 | tf_op jit(solution)/shard_map/ppermute | solution.py:129
  107.5 0.7 slice-start
  110.5 1.1 slice-start.1
  120.3 15.4 %copy-start.2 = (bf16[384,1280]{1,0:T(8,128)(2,1)S(1)}, bf16[384,1280]{1,0:T(8,128)(2,1)}, u32[]{:S(2)}) copy-start(bf16[384,1280]{1,0:T(8,128)(2,1)} %param.25) | copy-start | bytes 2949124
  134.9 0.8 copy-start.1
Sparse Core Ops, SparseCore 0:
  35.9 112.4 all-gather.2
  153.9 264.8 all-reduce.3
